TPU v7x, 256 devices: a whole 4x4x8 slice. The times are simulated.
256 devices in a mesh: vocab: 64 (over z, y, core), rows: 4 (over x).
Axes of the slice: x: 4, y: 4, z: 8, core: 2. Of those that a mesh axis runs over, the one named last changes fastest.
Arguments:
- hidden: bfloat16 [2048, 2880], P('rows'), may hold values from -60 to 60, as said below
- head_weight: bfloat16 [2880, 106496], P(None, ('vocab', 'rows')), may hold values from -0.1118034 to 0.1118034, as said below
- eta_level: float32 [2048], P('rows'), may hold values from 0.0001 to 0.003
Outputs:
- filtered_log: float32 [2048, 106496], P('rows', 'vocab')
- entropy: float32 [2048], P('rows')
Inputs may be any that keep to these rules, and one draw needn't show every extreme that they name: `hidden`: real-valued activations. `head_weight`: real-valued weights.
All inputs are finite; a program needn't handle non-finite values.
Results may differ from a plain program's by a relative error of at most 0.0003.
Values may be sent and summed in bfloat16 or wider, within the bound.
A program may use at most 64 MiB of HBM per device.

v0:
```python
import jax
import jax.numpy as jnp
from jax import lax
from jax.sharding import PartitionSpec as P


def from_everyone(shard, axis):
    peers = lax.axis_size(axis)
    return lax.all_to_all(
        jnp.broadcast_to(shard[None], (peers, *shard.shape)), axis, 0, 0, tiled=True
    )


def all_in_one(shard, axis):
    leaves = jax.tree.leaves(shard)
    sequence = sorted(range(len(leaves)), key=lambda k: -leaves[k].size)
    width = (1, *leaves[sequence[0]].shape)[-1]
    lines = [
        jnp.pad(leaves[k].reshape(-1), (0, -leaves[k].size % width)).reshape(-1, width)
        for k in sequence
    ]
    both, at, found = (from_everyone(jnp.concatenate(lines), axis), 0, {})
    for k, line in zip(sequence, lines):
        piece = both[:, at : at + len(line)].reshape(len(both), -1)
        found[k] = piece[:, : leaves[k].size].reshape(-1, *leaves[k].shape)
        at += len(line)
    numbers = iter(range(len(leaves)))
    return jax.tree.map(lambda _: found[next(numbers)], shard)


def combined_pairwise(pieces, combine):
    while len(jax.tree.leaves(pieces)[0]) > 1:
        pieces = jax.vmap(combine)(
            *(jax.tree.map(lambda part: part[side::2], pieces) for side in (0, 1))
        )
    return jax.tree.map(lambda part: part[0], pieces)


def joined_all(shard, axis, combine):
    pieces = all_in_one(shard, axis)
    return combined_pairwise(pieces, combine)


def over_copies(shard, axis):
    return from_everyone(shard, axis).sum(axis=0)


def combine_parts(first, second):
    first_peak, first_total, first_moment = first
    second_peak, second_total, second_moment = second
    top_peak = jnp.maximum(first_peak, second_peak)
    first_factor = jnp.exp(first_peak - top_peak)
    second_factor = jnp.exp(second_peak - top_peak)
    merged_total = first_total * first_factor + second_total * second_factor
    merged_moment = first_factor * (
        first_moment + (first_peak - top_peak) * first_total
    ) + second_factor * (second_moment + (second_peak - top_peak) * second_total)
    return (top_peak, merged_total, merged_moment)


def shards(hidden, head_weight, eta_level):
    scores = jnp.dot(
        hidden,
        lax.all_gather(head_weight, "rows", axis=1, tiled=True),
        preferred_element_type=jnp.float32,
    )
    local_peak = jnp.max(scores, axis=1)
    shifted = jnp.exp(scores - local_peak[:, None])
    local_total = jnp.sum(shifted, axis=1)
    local_moment = jnp.sum(shifted * (scores - local_peak[:, None]), axis=1)
    row_peak, row_total, moment = joined_all(
        (local_peak, local_total, local_moment), "vocab", combine_parts
    )
    shifted = shifted * jnp.exp(local_peak - row_peak)[:, None]
    entropy = jnp.log(row_total) - moment / row_total
    threshold = jnp.minimum(eta_level, jnp.sqrt(eta_level) * jnp.exp(-entropy))
    row_probs = shifted / row_total[:, None]
    kept_weight = jnp.maximum(row_probs - threshold[:, None], 0.0)
    kept_mass = over_copies(jnp.sum(kept_weight, axis=1), "vocab")
    filtered = jnp.log(kept_weight + 0.001 * threshold[:, None]) - jnp.log(kept_mass)[:, None]
    return (filtered, entropy)


def solution(mesh):
    return jax.shard_map(
        shards,
        mesh=mesh,
        in_specs=(P("rows", None), P(None, ("vocab", "rows")), P("rows")),
        out_specs=(P("rows", "vocab"), P("rows")),
        check_vma=False,
    )
```

profile of v0, /device:TPU:1, one launch (start us, length us, event | category | flops | bytes accessed | tf_op | source)
XLA Modules:
  0.0 188.1 jit_solution(3715837613669904508)
XLA Ops:
  7.2 0.0 copy-start
  7.2 0.0 all-gather.2.cloned.1.call-start
  7.2 0.7 all-gather.2.cloned.1.call-update
  7.9 103.3 %all-gather.2.cloned.1.call-done = bf16[2880,1664]{0,1:T(8,128)(2,1)} async-done(((bf16[2880,416]{0,1:T(8,128)(2,1)}), bf16[2880,1664]{0,1:T(8,128)(2,1)}) %all-gather.2.cloned.1.call-update) | async-done | bytes 9584656 | tf_op jit(solution)/shard_map/all_gather | solution.py:64
  111.2 0.0 copy-done
  111.2 9.8 %fusion.10 = (f32[512]{0:T(512)S(1)}, f32[512,1664]{1,0:T(8,128)S(1)}) fusion(bf16[512,2880]{0,1:T(8,128)(2,1)S(1)} %copy-done, bf16[2880,1664]{0,1:T(8,128)(2,1)} %all-gather.2.cloned.1.call-done), kind=kOutput, calls=%fused_computation.37 | convolution fusion | flops 4908187136 | bytes 15943680 | tf_op jit(solution)/shard_map/dot_general | solution.py:62
  121.0 0.0 copy-start.1
  121.1 1.7 copy-done.1
  122.8 1.0 exponential_reduce_fusion
  123.8 0.0 copy-start.2
  123.8 0.1 broadcast_in_dim.4
  123.9 28.2 %all_to_all.11 = f32[64,3,512]{2,1,0:T(4,128)S(1)} all-to-all(f32[64,3,512]{2,1,0:T(4,128)S(1)} %broadcast_in_dim.4), channel_id=1, replica_groups=mesh['vocab'=64,'rows'=4] {'vocab'}, dimensions={0} | all-to-all | bytes 786432 | tf_op jit(solution)/shard_map/all_to_all | solution.py:9
  152.1 0.3 fusion.9
  152.7 0.7 multiply_add_fusion
  153.4 0.8 slice.153
  154.2 0.8 slice.152
  155.7 0.0 copy-done.2
  155.7 0.6 broadcast_multiply_fusion
  156.3 3.8 %fusion.7 = (f32[512]{0:T(512)S(1)}, f32[512,1664]{1,0:T(8,128)}) fusion(f32[512]{0:T(512)S(1)} %get-tuple-element.5, f32[512]{0:T(512)S(1)} %bitcast.19, f32[512]{0:T(512)S(1)} %subtract_exponential_fusion, f32[512,1664]{1,0:T(8,128)} %copy-done.1, f32[512]{0:T(512)S(1)} %get-tuple-element.24), kind=kLoop, calls=%fused_computation.35 | loop fusion | flops 5111296 | bytes 6825984 | tf_op jit(solution)/shard_map/reduce_sum | solution.py:79
  160.2 0.1 broadcast_in_dim.5
  160.2 16.6 %all_to_all.12 = f32[64,1,512]{2,1,0:T(1,128)S(1)} all-to-all(f32[64,1,512]{2,1,0:T(1,128)S(1)} %broadcast_in_dim.5), channel_id=1, replica_groups=mesh['vocab'=64,'rows'=4] {'vocab'}, dimensions={0} | all-to-all | bytes 262144 | tf_op jit(solution)/shard_map/all_to_all | solution.py:9
  176.9 0.1 reduce_sum.39
  177.0 4.3 %log_subtract_fusion = f32[512,1664]{1,0:T(8,128)} fusion(f32[512,1664]{1,0:T(8,128)} %get-tuple-element.8, f32[512]{0:T(512)S(1)} %log.15, f32[512]{0:T(512)S(1)} %get-tuple-element.4), kind=kLoop, calls=%fused_computation.7 | loop fusion | flops 1703936 | bytes 6819840 | tf_op jit(solution)/shard_map/sub | solution.py:80
  (44 shorter events, 0.9 us)
Async XLA Ops:
  7.2 104.1 %copy-start = (bf16[512,2880]{0,1:T(8,128)(2,1)S(1)}, bf16[512,2880]{0,1:T(8,128)(2,1)}, u32[]{:S(2)}) copy-start(bf16[512,2880]{0,1:T(8,128)(2,1)} %param.3) | copy-start | bytes 8847364
  7.2 104.1 %all-gather.2.cloned.1.call-start = ((), (), s32[]{:S(2)}) async-start(), calls=%async_computation.2 | async-start | bytes 12247040 | tf_op jit(solution)/shard_map/all_gather | solution.py:64
  121.0 1.8 copy-start.1
  123.8 31.9 %copy-start.2 = (f32[512]{0:T(512)S(1)}, f32[512]{0:T(512)}, u32[]{:S(2)}) copy-start(f32[512]{0:T(512)} %param.5) | copy-start | bytes 6148
Sparse Core Ops, SparseCore 0:
  9.8 101.3 all-gather.1
where the time goes:
time: 188 us
  waiting for transfers between devices  104 us (55%)
  blocking collectives  44.8 us (24%)
  between operations  14.2 us (8%)
  other arithmetic  10.7 us (6%)
  matrix products  9.81 us (5%)
  local copies, waits for them, and re-layouts  4.51 us (2%)
    all_gather x1, waiting for transfers between devices, shards(): lax.all_gather(head_weight, 'rows', axis=1, tiled=True)  103 us
    all_to_all x2, blocking collectives, from_everyone(): lax.all_to_all(jnp.broadcast_to(shard[None], (peers, *shard.shape)), axis...  44.8 us
    dot_general x1, matrix products, shards(): jnp.dot(hidden, lax.all_gather(head_weight, 'rows', axis=1, tiled=True),...  9.81 us
    sub x1, other arithmetic, shards(): jnp.log(kept_weight + 0.001 * threshold[:, None])  4.27 us
    reduce_sum x1, other arithmetic, shards(): kept_mass = over_copies(jnp.sum(kept_weight, axis=1), 'vocab')  3.84 us
  transfers between devices with their start and end apart: 1, of which 1 were waited for; matrix products, arithmetic and copies ran while one was open for 0% of the time, Pallas kernels for 0%

commit v1 on v0

--- a/solution.py
+++ b/solution.py
@@ -2,6 +2,35 @@
 import jax.numpy as jnp
 from jax import lax
 from jax.sharding import PartitionSpec as P
+
+
+def supply_shifts_all(vals):
+    latest, mat_out, q_next = (lax.axis_size("rows"), lax.axis_index("rows"), vals.shape[1])
+    t_next = lax.dynamic_update_slice_in_dim(
+        jnp.zeros(
+            [dev_j * latest if idx == 1 else dev_j for idx, dev_j in enumerate(vals.shape)],
+            vals.dtype,
+        ),
+        vals,
+        mat_out * q_next,
+        axis=1,
+    )
+    r2 = taken_in = vals
+    for q in range(1, latest // 2 + 1):
+        r2 = lax.ppermute(
+            r2, axis_name="rows", perm=[(idx, (idx + 1) % latest) for idx in range(latest)]
+        )
+        t_next = lax.dynamic_update_slice_in_dim(
+            t_next, r2, (mat_out - q) % latest * q_next, axis=1
+        )
+        if 2 * q < latest:
+            taken_in = lax.ppermute(
+                taken_in, "rows", [(idx, (idx - 1) % latest) for idx in range(latest)]
+            )
+            t_next = lax.dynamic_update_slice_in_dim(
+                t_next, taken_in, (mat_out + q) % latest * q_next, axis=1
+            )
+    return t_next
 
 
 def from_everyone(shard, axis):
@@ -59,11 +88,7 @@
 
 
 def shards(hidden, head_weight, eta_level):
-    scores = jnp.dot(
-        hidden,
-        lax.all_gather(head_weight, "rows", axis=1, tiled=True),
-        preferred_element_type=jnp.float32,
-    )
+    scores = jnp.dot(hidden, supply_shifts_all(head_weight), preferred_element_type=jnp.float32)
     local_peak = jnp.max(scores, axis=1)
     shifted = jnp.exp(scores - local_peak[:, None])
     local_total = jnp.sum(shifted, axis=1)

time: 188 us -> 214 us (1.14)
  local copies, waits for them, and re-layouts: 4.51 us -> 33 us
  between operations: 14.2 us -> 0.85 us
  other arithmetic: 10.7 us -> 19.4 us
  waiting for transfers between devices: 104 us -> 97 us
  blocking collectives: 44.8 us -> 50.9 us
  starting transfers between devices: 0.04 us -> 5.36 us
  matrix products: 9.81 us -> 5.58 us
    all_gather x1 -> x0, waiting for transfers between devices: 103 us -> none  [shards(): lax.all_gather(head_weight, 'rows', axis=1, tiled=True)]
    ppermute x0 -> x3, waiting for transfers between devices: none -> 97 us  [the longest x2 97 us: supply_shifts_all(): lax.ppermute(r2, axis_name='rows', perm=[(idx, (idx + 1) % latest) for id...]
    slice x30, local copies, waits for them, and re-layouts: 2.3 us -> 18 us  [combined_pairwise(): part[side::2]]
    dynamic_update_slice x0 -> x4, local copies, waits for them, and re-layouts: none -> 6.42 us  [the longest x2 4.06 us: supply_shifts_all(): lax.dynamic_update_slice_in_dim(t_next, r2, (mat_out - q) % latest * q_ne...]
    all_to_all x2, blocking collectives: 44.8 us -> 50.9 us  [from_everyone(): lax.all_to_all(jnp.broadcast_to(shard[None], (peers, *shard.shape)), axis...]
    unnamed x7 -> x20, local copies, waits for them, and re-layouts: 1.77 us -> 7.52 us
    ppermute x0 -> x3, starting transfers between devices: none -> 5.36 us  [the longest x2 4 us: supply_shifts_all(): lax.ppermute(r2, axis_name='rows', perm=[(idx, (idx + 1) % latest) for id...]
    add x6, other arithmetic: 0.12 us -> 4.78 us  [combine_parts(): merged_total = first_total * first_factor + second_total * second_factor]
  transfers between devices with their start and end apart: 1 -> 3, of which waited for: 1 -> 2; matrix products, arithmetic and copies ran while one was open for 0% -> 2% of each run, Pallas kernels for 0% -> 0%
where the time goes in v1:
time: 214 us; the launch traced here: 212 us
  waiting for transfers between devices  97 us (45%)
  blocking collectives  50.9 us (24%)
  local copies, waits for them, and re-layouts  33 us (15%)
  other arithmetic  19.4 us (9%)
  matrix products  5.58 us (3%)
  starting transfers between devices  5.36 us (3%)
    ppermute x2, waiting for transfers between devices, supply_shifts_all(): lax.ppermute(r2, axis_name='rows', perm=[(idx, (idx + 1) % latest) for id...  97 us
    all_to_all x2, blocking collectives, from_everyone(): lax.all_to_all(jnp.broadcast_to(shard[None], (peers, *shard.shape)), axis...  50.9 us
    slice x30, local copies, waits for them, and re-layouts, combined_pairwise(): part[side::2]  18 us
    unnamed x20, local copies, waits for them, and re-layouts  7.52 us
    dot_general x1, matrix products, shards(): jnp.dot(hidden, supply_shifts_all(head_weight), preferred_element_type=jn...  5.58 us
    sub x1, other arithmetic, shards(): jnp.log(kept_weight + 0.001 * threshold[:, None])  4.91 us
    add x6, other arithmetic, combine_parts(): merged_total = first_total * first_factor + second_total * second_factor  4.78 us
  transfers between devices with their start and end apart: 3, of which 2 were waited for; matrix products, arithmetic and copies ran while one was open for 2% of the time, Pallas kernels for 0%

profile of v1, /device:TPU:1, one launch (start us, length us, event | category | flops | bytes accessed | tf_op | source)
XLA Modules:
  0.0 212.2 jit_solution(1075750705874465031)
XLA Ops:
  0.6 0.0 copy-start
  0.6 2.1 collective-permute-start
  2.8 1.4 collective-permute-start.1
  4.1 50.8 %collective-permute-done = bf16[2880,416]{0,1:T(8,128)(2,1)} collective-permute-done((bf16[2880,416]{0,1:T(8,128)(2,1)}, bf16[2880,416]{0,1:T(8,128)(2,1)}, u32[]{:S(2)}, u32[]{:S(2)}) %collective-permute-start) | collective-permute-done | bytes 2396192 | tf_op jit(solution)/shard_map/ppermute | solution.py:20
  55.0 1.9 collective-permute-start.2
  56.8 0.0 copy-start.2
  56.8 0.7 broadcast_in_dim.6
  57.5 1.0 copy-done.2
  58.5 0.3 constant_dynamic-update-slice_fusion.3
  58.9 2.0 constant_dynamic-update-slice_fusion.2
  60.9 0.0 collective-permute-done.1
  60.9 2.0 constant_dynamic-update-slice_fusion.1
  62.9 46.2 %collective-permute-done.2 = bf16[2880,416]{0,1:T(8,128)(2,1)} collective-permute-done((bf16[2880,416]{0,1:T(8,128)(2,1)}, bf16[2880,416]{0,1:T(8,128)(2,1)}, u32[]{:S(2)}, u32[]{:S(2)}) %collective-permute-start.2) | collective-permute-done | bytes 2396192 | tf_op jit(solution)/shard_map/ppermute | solution.py:20
  109.2 2.0 constant_dynamic-update-slice_fusion
  111.2 0.0 copy-done
  111.2 5.6 %fusion.9 = (f32[512]{0:T(512)S(1)}, f32[1664,512]{1,0:T(8,128)S(1)}) fusion(bf16[2880,1664]{0,1:T(8,128)(2,1)S(1)} %constant_dynamic-update-slice_fusion, bf16[512,2880]{0,1:T(8,128)(2,1)S(1)} %copy-done), kind=kOutput, calls=%fused_computation.41 | convolution fusion | flops 4908187136 | bytes 15943680 | tf_op jit(solution)/shard_map/dot_general | solution.py:91
  116.8 0.0 copy-start.1
  116.8 0.0 copy-start.7
  116.8 1.7 copy-done.1
  118.5 0.7 exponential_reduce_fusion
  119.3 0.1 broadcast_in_dim.7
  119.3 34.3 %all_to_all.11 = f32[64,3,512]{2,1,0:T(4,128)S(1)} all-to-all(f32[64,3,512]{2,1,0:T(4,128)S(1)} %broadcast_in_dim.7), channel_id=1, replica_groups=mesh['vocab'=64,'rows'=4] {'vocab'}, dimensions={0} | all-to-all | bytes 786432 | tf_op jit(solution)/shard_map/all_to_all | solution.py:38
  153.6 0.3 fusion.8
  153.9 0.0 copy-done.7
  154.0 0.7 multiply_add_fusion.1
  154.7 0.0 copy-start.3
  154.7 0.0 copy-start.4
  154.8 0.9 slice.139
  155.6 0.9 slice.140
  156.5 0.6 multiply_add_fusion.3
  157.1 0.8 slice.128
  157.9 1.4 slice.129
  159.2 1.4 slice.141
  160.6 1.4 slice.142
  162.0 1.4 multiply_add_fusion.5
  163.3 1.3 slice.130
  164.7 1.3 slice.131
  166.0 1.3 slice.143
  167.3 1.3 slice.144
  168.6 1.4 multiply_add_fusion.7
  170.0 1.3 slice.132
  171.3 1.3 slice.133
  172.6 1.3 slice.145
  173.9 1.3 slice.146
  175.2 0.0 copy-done.3
  175.2 0.0 copy-done.4
  175.2 0.0 copy-done.5
  175.2 0.0 copy-done.6
  175.2 0.6 slice.151
  175.9 0.9 multiply_add_fusion
  176.8 0.8 multiply_add_fusion.2
  177.7 0.8 multiply_add_fusion.4
  178.5 0.8 multiply_add_fusion.6
  179.4 0.7 multiply_add_fusion.9
  180.1 0.7 subtract_exponential_fusion
  180.8 0.7 multiply_add_fusion.8
  181.6 1.3 broadcast_multiply_fusion
  182.9 2.9 %fusion.4 = f32[512]{0:T(512)S(1)} fusion(f32[512]{0:T(512)S(1)} %get-tuple-element.11, f32[512]{0:T(512)S(1)} %bitcast.27, f32[512]{0:T(512)S(1)} %subtract_exponential_fusion, f32[1664,512]{1,0:T(8,128)} %copy-done.1, f32[512]{0:T(512)} %copy-done.7), kind=kLoop, calls=%fused_computation.8 | loop fusion | flops 5111296 | bytes 3418112 | tf_op jit(solution)/shard_map/reduce_sum | solution.py:104
  185.7 0.1 broadcast_in_dim.8
  185.8 16.6 %all_to_all.12 = f32[64,1,512]{2,1,0:T(1,128)S(1)} all-to-all(f32[64,1,512]{2,1,0:T(1,128)S(1)} %broadcast_in_dim.8), channel_id=1, replica_groups=mesh['vocab'=64,'rows'=4] {'vocab'}, dimensions={0} | all-to-all | bytes 262144 | tf_op jit(solution)/shard_map/all_to_all | solution.py:38
  202.4 0.1 reduce_sum.39
  202.6 0.0 copy-done.8
  202.6 4.9 %log_subtract_fusion = f32[512,1664]{0,1:T(8,128)} fusion(f32[512]{0:T(512)S(1)} %log.15, f32[512]{0:T(512)S(1)} %get-tuple-element.10, f32[512]{0:T(512)S(1)} %get-tuple-element.11, f32[512]{0:T(512)S(1)} %bitcast.28, f32[512]{0:T(512)S(1)} %subtract_exponential_fusion, f32[1664,512]{1,0:T(8,128)} %copy-done.1, f32[512]{0:T(512)S(1)} %copy-done.8), kind=kLoop, calls=%fused_computation.7 | loop fusion | flops 5963776 | bytes 6828032 | tf_op jit(solution)/shard_map/sub | solution.py:105
  207.5 4.7 %copy.14 = f32[512,1664]{1,0:T(8,128)} copy(f32[512,1664]{0,1:T(8,128)} %log_subtract_fusion) | data formatting | bytes 6815744
  (24 shorter events, 0.4 us)
Async XLA Ops:
  0.6 110.6 %copy-start = (bf16[512,2880]{0,1:T(8,128)(2,1)S(1)}, bf16[512,2880]{0,1:T(8,128)(2,1)}, u32[]{:S(2)}) copy-start(bf16[512,2880]{0,1:T(8,128)(2,1)} %param.3) | copy-start | bytes 8847364
  0.6 54.3 %collective-permute-start = (bf16[2880,416]{0,1:T(8,128)(2,1)}, bf16[2880,416]{0,1:T(8,128)(2,1)}, u32[]{:S(2)}, u32[]{:S(2)}) collective-permute-start(bf16[2880,416]{0,1:T(8,128)(2,1)} %param.4), channel_id=1, source_target_pairs={{0,1},{1,2},{2,3},{3,0},{4,5},{5,6},{6,7},{7,4},{8,9},{9,10},{10,1... | collective-permute-start | bytes 7188488 | tf_op jit(solution)/shard_map/ppermute | solution.py:20
  2.8 58.1 %collective-permute-start.1 = (bf16[2880,416]{0,1:T(8,128)(2,1)}, bf16[2880,416]{0,1:T(8,128)(2,1)}, u32[]{:S(2)}, u32[]{:S(2)}) collective-permute-start(bf16[2880,416]{0,1:T(8,128)(2,1)} %param.4), channel_id=1, source_target_pairs={{0,3},{1,0},{2,1},{3,2},{4,7},{5,4},{6,5},{7,6},{8,11},{9,8},{10,9... | collective-permute-start | bytes 7188488 | tf_op jit(solution)/shard_map/ppermute | solution.py:27
  55.0 54.2 %collective-permute-start.2 = (bf16[2880,416]{0,1:T(8,128)(2,1)}, bf16[2880,416]{0,1:T(8,128)(2,1)}, u32[]{:S(2)}, u32[]{:S(2)}) collective-permute-start(bf16[2880,416]{0,1:T(8,128)(2,1)} %collective-permute-done), channel_id=1, source_target_pairs={{0,1},{1,2},{2,3},{3,0},{4,5},{5,6},{6,7},{7,4},{8,9},{9,10},{10,1... | collective-permute-start | bytes 7188488 | tf_op jit(solution)/shard_map/ppermute | solution.py:20
  56.8 1.7 copy-start.2
  116.8 1.8 copy-start.1
  116.8 37.1 %copy-start.7 = (f32[512]{0:T(512)}, f32[512]{0:T(512)S(1)}, u32[]{:S(2)}) copy-start(f32[512]{0:T(512)S(1)} %get-tuple-element.28) | copy-start | bytes 6148
  154.7 20.4 %copy-start.3 = (f32[16,512]{1,0:T(8,128)}, f32[16,512]{1,0:T(8,128)S(1)}, u32[]{:S(2)}) copy-start(f32[16,512]{1,0:T(8,128)S(1)} %slice.126) | copy-start | bytes 98308
  154.7 20.4 %copy-start.4 = (f32[16,512]{1,0:T(8,128)}, f32[16,512]{1,0:T(8,128)S(1)}, u32[]{:S(2)}) copy-start(f32[16,512]{1,0:T(8,128)S(1)} %slice.127) | copy-start | bytes 98308
  155.6 19.5 %copy-start.5 = (f32[16,512]{1,0:T(8,128)}, f32[16,512]{1,0:T(8,128)S(1)}, u32[]{:S(2)}) copy-start(f32[16,512]{1,0:T(8,128)S(1)} %slice.139) | copy-start | bytes 98308
  156.5 18.7 %copy-start.6 = (f32[16,512]{1,0:T(8,128)}, f32[16,512]{1,0:T(8,128)S(1)}, u32[]{:S(2)}) copy-start(f32[16,512]{1,0:T(8,128)S(1)} %slice.140) | copy-start | bytes 98308
  175.9 26.7 %copy-start.8 = (f32[512]{0:T(512)S(1)}, f32[512]{0:T(512)}, u32[]{:S(2)}) copy-start(f32[512]{0:T(512)} %copy-done.7) | copy-start | bytes 6148
